TPU v7x, 32 devices: a whole 2x2x4 slice. The times are simulated.
32 devices in a mesh: parts: 2 (over y), freq: 4 (over x, core), sx: 4 (over z).
Axes of the slice: x: 2, y: 2, z: 4, core: 2. Of those that a mesh axis runs over, the one named last changes fastest.
Arguments:
- design_density: float32 [64, 8, 1024], P(None, 'sx', 'parts'), parts along dimension 2, may hold values from 0.3 to 1
- observation: float32 [64, 8, 1024], P(None, 'sx', 'parts'), parts along dimension 2, may hold values from 0.1 to 1
- source: float32 [64, 8, 1024], P(None, 'sx', 'parts'), parts along dimension 2, may hold values from -6 to 6
- amplitude: float32 [8, 2], P('freq'), may hold values from -1 to 1
- omega_sq: float32 [8], P('freq'), may hold values from 0.5 to 2
- coupling: float32 [7, 64, 64], replicated, may hold values from -0.25 to 0.25
- inverse_blocks: float32 [8, 2, 64, 64], P('freq'), may hold values from -0.375 to 0.375
- primal_field: float32 [8, 2, 64, 8, 1024], P('freq', None, None, 'sx', 'parts'), parts along dimension 4, may hold values from -6 to 6
- adjoint_field: float32 [8, 2, 64, 8, 1024], P('freq', None, None, 'sx', 'parts'), parts along dimension 4, may hold values from -6 to 6
Outputs:
- density_gradient: float32 [64, 8, 1024], P('freq', 'sx', 'parts'), parts along dimension 2
There are 2 independent parts, one for each index of `parts`. A program takes and returns all parts, laid end to end along the dimension named above; an argument that names none is the same for every part. Nothing has to cross between parts.
All inputs are finite; a program needn't handle non-finite values.
Results may differ from a plain program's by a relative error of at most 0.0001.
Values sent between devices are 32-bit elements; how exact they have to be, the bound alone decides.
A program may use at most 64 MiB of HBM per device.

v0:
```python
import functools

import jax
import jax.numpy as jnp
from jax import lax
from jax.experimental import pallas as pl
from jax.experimental.pallas import tpu as pltpu
from jax.sharding import PartitionSpec as P

BZ = 32
BETA = 0.5
MESH = pl.DeviceIdType.MESH
PIECES = 2


def split(v):
    hi = v.astype(jnp.bfloat16)
    lo = (v - hi.astype(jnp.float32)).astype(jnp.bfloat16)
    return hi, lo


def left_operand(m):
    hi, lo = split(m)
    return jnp.concatenate(
        [jnp.concatenate([hi, hi], axis=1), jnp.concatenate([lo, jnp.zeros_like(lo)], axis=1)], axis=0
    )


def folded_dot(left, right):
    r = jnp.dot(left, right, preferred_element_type=jnp.float32)
    half = r.shape[0] // 2
    return r[:half] + r[half:]


def kernel(
    nf, nsx,
    amp, om, den_h, obs_h, src_h, cpl, inv, p_h, a_h,
    out_h,
    den, obs, src, p, a, sp, pn, an, rp, ra, hal, lk, lh, lp, grad, got, osum,
    small_sem, field_sem, send_h, recv_h, send_g, recv_g, out_sem,
):
    F, X, _, Q, N = p.shape
    rows = Q // nf
    me_f, me_s = lax.axis_index("freq"), lax.axis_index("sx")
    has = (me_s > 0, me_s < nsx - 1)

    smalls = []
    for i, (h, v) in enumerate(((den_h, den), (obs_h, obs), (src_h, src))):
        smalls.append([pltpu.make_async_copy(h.at[:, x, :], v.at[x], small_sem.at[i, x]) for x in range(X)])
    fields = [
        [[pltpu.make_async_copy(h.at[f, :, :, x, :], v.at[f, x], field_sem.at[i, f, x]) for x in range(X)] for f in range(F)]
        for i, (h, v) in enumerate(((p_h, p), (a_h, a)))
    ]

    def start(copies):
        for c in copies:
            c.start()

    def wait(copies):
        for c in copies:
            c.wait()

    start(fields[1][0])
    start(smalls[0])
    start(fields[0][0])
    start(fields[1][1])
    start(fields[0][1])
    start(smalls[2])
    start(smalls[1])

    barrier = pltpu.get_barrier_semaphore()
    for k in range(1, nf):
        pl.semaphore_signal(barrier, inc=1, device_id={"freq": lax.rem(me_f + k, nf)}, device_id_type=MESH)

    @pl.when(has[0])
    def _():
        pl.semaphore_signal(barrier, inc=1, device_id={"sx": me_s - 1}, device_id_type=MESH)

    @pl.when(has[1])
    def _():
        pl.semaphore_signal(barrier, inc=1, device_id={"sx": me_s + 1}, device_id_type=MESH)

    pl.semaphore_wait(barrier, nf - 1 + has[0].astype(jnp.int32) + has[1].astype(jnp.int32))

    def halo_copy(kind, f, side, piece=None):
        v = (a, sp, an)[kind]
        x, to = (X - 1, me_s + 1) if side == 0 else (0, me_s - 1)
        s, d = v.at[f, x], hal.at[kind, f, side]
        if piece is not None:
            cols = pl.ds(piece * (N // PIECES), N // PIECES)
            s, d = s.at[:, :, cols], d.at[:, :, cols]
        n = piece or 0
        return pltpu.make_async_remote_copy(
            src_ref=s, dst_ref=d, send_sem=send_h.at[kind, f, side, n], recv_sem=recv_h.at[kind, f, side, n],
            device_id={"sx": to}, device_id_type=MESH,
        )

    def halo(kind, f, do, piece=None):
        for side in range(2):
            there = has[side] if do == "wait_recv" else has[1 - side]

            @pl.when(there)
            def _():
                getattr(halo_copy(kind, f, side, piece), do)()

    def stiff(x):
        d = den[x]
        return d * d * d

    for f in range(F):
        wait(fields[1][f])
        halo(0, f, "start")
        if f == 0:
            wait(smalls[0])
        wait(fields[0][f])
        for x in range(X):
            s = stiff(x)
            for c in range(2):
                sp[f, x, c] = s * p[f, x, c]
        halo(1, f, "start")

    for side in range(2):

        @pl.when(jnp.logical_not(has[side]))
        def _():
            for kind in range(3):
                for f in range(F):
                    hal[kind, f, side] = jnp.zeros((2, Q, N), jnp.float32)

    cs = [cpl[d] for d in range(7)]
    ct = [c.T for c in cs]
    for j, order in enumerate((
        (cs[0], cs[3], cs[4], cs[5], cs[6], (cs[2], cs[1])),
        (ct[0], ct[4], ct[3], ct[6], ct[5], (ct[1], ct[2])),
    )):
        common = [left_operand(m) for m in order[:5]]
        other = [left_operand(m) for m in order[5]]
        for x in range(X):
            lk[j, x] = jnp.concatenate(common + [other[x]], axis=1)
            lh[j, x] = other[1 - x]
    for f in range(F):
        re, im = inv[f, 0], inv[f, 1]
        for j, (r, i) in enumerate(((re, im), (re.T, im.T))):
            lp[j, f] = left_operand(
                jnp.concatenate([jnp.concatenate([r, -i], axis=1), jnp.concatenate([i, r], axis=1)], axis=0)
            )

    column = lax.broadcasted_iota(jnp.int32, (Q, N), 1)
    place = column % BZ

    def local_sum(j, v, f, x, c):
        own, other = v[f, x, c], v[f, 1 - x, c]
        parts = [
            own,
            jnp.where(column >= BZ, pltpu.roll(own, BZ, 1), 0.0),
            jnp.where(column < N - BZ, pltpu.roll(own, N - BZ, 1), 0.0),
            jnp.where(place != 0, pltpu.roll(own, 1, 1), 0.0),
            jnp.where(place != BZ - 1, pltpu.roll(own, N - 1, 1), 0.0),
            other,
        ]
        right = jnp.concatenate([h for m in parts for h in split(m)], axis=0)
        return folded_dot(lk[j, x], right)

    def halo_sum(j, values, x):
        return folded_dot(lh[j, x], jnp.concatenate(split(values), axis=0))

    def mass(w, re, im):
        return w * (re + BETA * im), w * (im - BETA * re)

    wait(smalls[2])

    def residuals(i, carry):
        f, x = i // X, i % X
        d = den[x]
        w = om[f] * d
        mp = mass(w, p[f, x, 0], p[f, x, 1])
        ma = mass(w, a[f, x, 0], a[f, x, 1])
        s = d * d * d
        for c in range(2):
            rp[f, x, c] = amp[f, c] * src[x] - local_sum(0, sp, f, x, c) + mp[c]
            ra[f, x, c] = ma[c] - s * local_sum(1, a, f, x, c)
        return carry

    lax.fori_loop(0, F * X, residuals, 0)
    wait(smalls[1])

    for f in range(F):
        halo(0, f, "wait_recv")
        halo(1, f, "wait_recv")

        def sweep(x, carry, f=f):
            r = [rp[f, x, c] - halo_sum(0, hal[1, f, x, c], x) for c in range(2)]
            step = folded_dot(lp[0, f], jnp.concatenate(split(jnp.concatenate(r, axis=0)), axis=0))
            new = [p[f, x, c] + step[c * Q:(c + 1) * Q] for c in range(2)]
            s, o = stiff(x), obs[x]
            r = [ra[f, x, c] - s * halo_sum(1, hal[0, f, x, c], x) - o * new[c] for c in range(2)]
            step = folded_dot(lp[1, f], jnp.concatenate(split(jnp.concatenate(r, axis=0)), axis=0))
            for c in range(2):
                pn[f, x, c] = new[c]
                an[f, x, c] = a[f, x, c] + step[c * Q:(c + 1) * Q]
            return carry

        lax.fori_loop(0, X, sweep, 0)
        for piece in range(PIECES):
            halo(2, f, "start", piece)

    def gradient(x, carry):
        d = den[x]
        three = 3.0 * d * d
        total = jnp.zeros((Q, N), jnp.float32)
        for f in range(F):
            pr, pi, ar, ai = pn[f, x, 0], pn[f, x, 1], an[f, x, 0], an[f, x, 1]
            wr, wi = local_sum(1, an, f, x, 0), local_sum(1, an, f, x, 1)
            total = total + three * (pr * wr - pi * wi)
            total = total - om[f] * ((ar * pr - ai * pi) + BETA * (ar * pi + ai * pr))
        grad[x] = total
        return carry

    lax.fori_loop(0, X, gradient, 0)

    def share(k, piece):
        peer = lax.rem(me_f + k, nf)
        cols = pl.ds(piece * (N // PIECES), N // PIECES)
        return pltpu.make_async_remote_copy(
            src_ref=grad.at[:, pl.ds(pl.multiple_of(peer * rows, rows), rows), cols],
            dst_ref=got.at[k - 1, :, :, cols],
            send_sem=send_g.at[k - 1, piece], recv_sem=recv_g.at[k - 1, piece],
            device_id={"freq": peer}, device_id_type=MESH,
        )

    for f in range(F):
        for piece in range(PIECES):
            cols = slice(piece * (N // PIECES), (piece + 1) * (N // PIECES))
            halo(2, f, "wait_recv", piece)
            for x in range(X):
                d = den[x, :, cols]
                h = [halo_sum(1, hal[2, f, x, c, :, cols], x) for c in range(2)]
                grad[x, :, cols] += (3.0 * d * d) * (pn[f, x, 0, :, cols] * h[0] - pn[f, x, 1, :, cols] * h[1])
            if f == F - 1:
                for k in range(1, nf):
                    share(k, piece).start()

    mine = pl.ds(pl.multiple_of(me_f * rows, rows), rows)
    for piece in range(PIECES):
        cols = slice(piece * (N // PIECES), (piece + 1) * (N // PIECES))
        total = grad[:, mine, cols]
        for k in range(1, nf):
            share(k, piece).wait_recv()
            total = total + got[k - 1, :, :, cols]
        osum[:, :, cols] = total
    outs = [pltpu.make_async_copy(osum.at[x], out_h.at[:, x, :], out_sem.at[x]) for x in range(X)]
    start(outs)
    wait(outs)
    for f in range(F):
        halo(0, f, "wait_send")
        halo(1, f, "wait_send")
        for piece in range(PIECES):
            halo(2, f, "wait_send", piece)
    for piece in range(PIECES):
        for k in range(1, nf):
            share(k, piece).wait_send()


def shards(nf, nsx, den, obs, src, amp, om, cpl, inv, p, a):
    F, _, Q, X, N = p.shape
    rows = Q // nf
    f32, bf16, dma = jnp.float32, jnp.bfloat16, pltpu.SemaphoreType.DMA
    field = pltpu.VMEM((F, X, 2, Q, N), f32)
    plane = pltpu.VMEM((X, Q, N), f32)
    smem = pl.BlockSpec(memory_space=pltpu.SMEM)
    vmem = pl.BlockSpec(memory_space=pltpu.VMEM)
    anyw = pl.BlockSpec(memory_space=pl.ANY)
    columns = F * X * 2 * N
    return pl.pallas_call(
        functools.partial(kernel, nf, nsx),
        out_shape=jax.ShapeDtypeStruct((rows, X, N), f32),
        in_specs=[smem, smem, anyw, anyw, anyw, vmem, vmem, anyw, anyw],
        out_specs=anyw,
        scratch_shapes=[
            plane, plane, plane,
            field, field, field, field, field, field, field,
            pltpu.VMEM((3, F, 2, 2, Q, N), f32),
            pltpu.VMEM((2, X, 2 * Q, 12 * Q), bf16),
            pltpu.VMEM((2, X, 2 * Q, 2 * Q), bf16),
            pltpu.VMEM((2, F, 4 * Q, 4 * Q), bf16),
            plane,
            pltpu.VMEM((nf - 1, X, rows, N), f32),
            pltpu.VMEM((X, rows, N), f32),
            dma((3, X)), dma((2, F, X)),
            dma((3, F, 2, PIECES)), dma((3, F, 2, PIECES)),
            dma((nf - 1, PIECES)), dma((nf - 1, PIECES)),
            dma((X,)),
        ],
        compiler_params=pltpu.CompilerParams(
            collective_id=0, has_side_effects=True, vmem_limit_bytes=48 * 1024 * 1024
        ),
        cost_estimate=pl.CostEstimate(
            flops=2 * columns * (3 * 7 * Q * Q + 4 * Q * Q) * 3, bytes_accessed=4 * (2 * columns * Q), transcendentals=0
        ),
    )(amp, om, den, obs, src, cpl, inv, p, a)


def solution(mesh):
    in_specs = (
        P(None, "sx", "parts"),
        P(None, "sx", "parts"),
        P(None, "sx", "parts"),
        P("freq", None),
        P("freq"),
        P(),
        P("freq", None, None, None),
        P("freq", None, None, "sx", "parts"),
        P("freq", None, None, "sx", "parts"),
    )
    out_specs = P("freq", "sx", "parts")
    body = functools.partial(shards, mesh.shape["freq"], mesh.shape["sx"])
    return jax.shard_map(body, mesh=mesh, in_specs=in_specs, out_specs=out_specs, check_vma=False)
```

profile of v0, /device:TPU:0, one launch (start us, length us, event | category | flops | bytes accessed | tf_op | source)
XLA Modules:
  0.0 54.8 jit_solution(10861489014938486196)
XLA Ops:
  0.0 0.0 copy-start
  0.0 1.2 %copy-done = f32[2,2,64,2,512]{4,3,2,1,0:T(2,128)S(1)} copy-done((f32[2,2,64,2,512]{4,3,2,1,0:T(2,128)S(1)}, f32[2,2,64,2,512]{4,3,2,1,0:T(2,128)}, u32[]{:S(2)}) %copy-start) | copy-done | bytes 1048600
  1.2 0.0 copy-start.1
  1.2 1.2 %copy-done.1 = f32[2,2,64,2,512]{4,3,2,1,0:T(2,128)S(1)} copy-done((f32[2,2,64,2,512]{4,3,2,1,0:T(2,128)S(1)}, f32[2,2,64,2,512]{4,3,2,1,0:T(2,128)}, u32[]{:S(2)}) %copy-start.1) | copy-done | bytes 1048600
  2.5 0.0 copy-start.2
  2.5 0.9 %copy-done.2 = f32[64,2,512]{2,1,0:T(2,128)S(1)} copy-done((f32[64,2,512]{2,1,0:T(2,128)S(1)}, f32[64,2,512]{2,1,0:T(2,128)}, u32[]{:S(2)}) %copy-start.2) | copy-done | bytes 262168
  3.4 0.0 copy-start.3
  3.4 0.9 %copy-done.3 = f32[64,2,512]{2,1,0:T(2,128)S(1)} copy-done((f32[64,2,512]{2,1,0:T(2,128)S(1)}, f32[64,2,512]{2,1,0:T(2,128)}, u32[]{:S(2)}) %copy-start.3) | copy-done | bytes 262168
  4.4 0.0 copy-start.4
  4.4 0.9 %copy-done.4 = f32[64,2,512]{2,1,0:T(2,128)S(1)} copy-done((f32[64,2,512]{2,1,0:T(2,128)S(1)}, f32[64,2,512]{2,1,0:T(2,128)}, u32[]{:S(2)}) %copy-start.4) | copy-done | bytes 262168
  5.3 0.0 copy-start.5
  5.3 0.9 %copy-done.5 = f32[7,64,64]{2,1,0:T(8,128)S(1)} copy-done((f32[7,64,64]{2,1,0:T(8,128)S(1)}, f32[7,64,64]{2,1,0:T(8,128)}, u32[]{:S(2)}) %copy-start.5) | copy-done | bytes 114712
  6.2 0.0 copy-start.6
  6.2 0.9 %copy-done.6 = f32[2,2,64,64]{3,2,1,0:T(8,128)S(1)} copy-done((f32[2,2,64,64]{3,2,1,0:T(8,128)S(1)}, f32[2,2,64,64]{3,2,1,0:T(8,128)}, u32[]{:S(2)}) %copy-start.6) | copy-done | bytes 65560
  7.1 0.0 copy-start.7
  7.1 0.7 %copy-done.7 = f32[2,2]{1,0:T(2,128)S(1)} copy-done((f32[2,2]{1,0:T(2,128)S(1)}, f32[2,2]{1,0:T(2,128)}, u32[]{:S(2)}) %copy-start.7) | copy-done | bytes 40
  7.8 0.0 copy-start.8
  7.8 0.7 %copy-done.8 = f32[2]{0:T(128)S(1)} copy-done((f32[2]{0:T(128)S(1)}, f32[2]{0:T(128)}, u32[]{:S(2)}) %copy-start.8) | copy-done | bytes 32
  8.5 45.6 %shard_map.91 = f32[16,2,512]{2,1,0:T(2,128)S(1)} custom-call(f32[2,2]{1,0:T(2,128)S(1)} %copy-done.7, f32[2]{0:T(128)S(1)} %copy-done.8, f32[64,2,512]{2,1,0:T(2,128)S(1)} %copy-done.2, f32[64,2,512]{2,1,0:T(2,128)S(1)} %copy-done.3, f32[64,2,512]{2,1,0:T(2,128)S(1)} %copy-done.4, f32[7,64,64]{2,1,0:T(8,128)S(1)} %copy-done.5, ...), custom_call_target="tpu_custom_call" | custom-call | flops 2516582400 | bytes 2097152 | tf_op jit(solution)/shard_map/pallas_call | solution.py:274
  54.1 0.6 %copy.11 = f32[16,2,512]{2,1,0:T(2,128)} copy(f32[16,2,512]{2,1,0:T(2,128)S(1)} %shard_map.91) | data formatting | bytes 131072
Async XLA Ops:
  0.0 1.2 %copy-start = (f32[2,2,64,2,512]{4,3,2,1,0:T(2,128)S(1)}, f32[2,2,64,2,512]{4,3,2,1,0:T(2,128)}, u32[]{:S(2)}) copy-start(f32[2,2,64,2,512]{4,3,2,1,0:T(2,128)} %p_h.1) | copy-start | bytes 3145732
  1.2 1.2 %copy-start.1 = (f32[2,2,64,2,512]{4,3,2,1,0:T(2,128)S(1)}, f32[2,2,64,2,512]{4,3,2,1,0:T(2,128)}, u32[]{:S(2)}) copy-start(f32[2,2,64,2,512]{4,3,2,1,0:T(2,128)} %a_h.1) | copy-start | bytes 3145732
  2.5 0.9 %copy-start.2 = (f32[64,2,512]{2,1,0:T(2,128)S(1)}, f32[64,2,512]{2,1,0:T(2,128)}, u32[]{:S(2)}) copy-start(f32[64,2,512]{2,1,0:T(2,128)} %den_h.1) | copy-start | bytes 786436
  3.4 0.9 %copy-start.3 = (f32[64,2,512]{2,1,0:T(2,128)S(1)}, f32[64,2,512]{2,1,0:T(2,128)}, u32[]{:S(2)}) copy-start(f32[64,2,512]{2,1,0:T(2,128)} %obs_h.1) | copy-start | bytes 786436
  4.4 0.9 %copy-start.4 = (f32[64,2,512]{2,1,0:T(2,128)S(1)}, f32[64,2,512]{2,1,0:T(2,128)}, u32[]{:S(2)}) copy-start(f32[64,2,512]{2,1,0:T(2,128)} %src_h.1) | copy-start | bytes 786436
  5.3 0.9 %copy-start.5 = (f32[7,64,64]{2,1,0:T(8,128)S(1)}, f32[7,64,64]{2,1,0:T(8,128)}, u32[]{:S(2)}) copy-start(f32[7,64,64]{2,1,0:T(8,128)} %cpl.1) | copy-start | bytes 344068
  6.2 0.9 %copy-start.6 = (f32[2,2,64,64]{3,2,1,0:T(8,128)S(1)}, f32[2,2,64,64]{3,2,1,0:T(8,128)}, u32[]{:S(2)}) copy-start(f32[2,2,64,64]{3,2,1,0:T(8,128)} %inv.1) | copy-start | bytes 196612
  7.1 0.7 %copy-start.7 = (f32[2,2]{1,0:T(2,128)S(1)}, f32[2,2]{1,0:T(2,128)}, u32[]{:S(2)}) copy-start(f32[2,2]{1,0:T(2,128)} %amp.1) | copy-start | bytes 52
  7.8 0.7 %copy-start.8 = (f32[2]{0:T(128)S(1)}, f32[2]{0:T(128)}, u32[]{:S(2)}) copy-start(f32[2]{0:T(128)} %om.1) | copy-start | bytes 28
where the time goes:
time: 55.1 us; the launch traced here: 54.8 us
  Pallas kernels  45.6 us (83%)
  local copies, waits for them, and re-layouts  9.1 us (17%)
    pallas_call x1, Pallas kernels, shards(): pl.pallas_call(functools.partial(kernel, nf, nsx), out_shape=jax.ShapeDty...  45.6 us
    unnamed x19, local copies, waits for them, and re-layouts  9.1 us

commit v1 on v0

--- a/solution.py
+++ b/solution.py
@@ -34,10 +34,11 @@
 
 def kernel(
     nf, nsx,
-    amp, om, den_h, obs_h, src_h, cpl, inv, p_h, a_h,
+    amp_h, om_h, den_h, obs_h, src_h, cpl_h, inv_h, p_h, a_h,
     out_h,
+    amp, om, cpl, inv,
     den, obs, src, p, a, sp, pn, an, rp, ra, hal, lk, lh, lp, grad, got, osum,
-    small_sem, field_sem, send_h, recv_h, send_g, recv_g, out_sem,
+    param_sem, small_sem, field_sem, send_h, recv_h, send_g, recv_g, out_sem,
 ):
     F, X, _, Q, N = p.shape
     rows = Q // nf
@@ -52,6 +53,11 @@
         for i, (h, v) in enumerate(((p_h, p), (a_h, a)))
     ]
 
+    params = [
+        pltpu.make_async_copy(h, v, param_sem.at[i])
+        for i, (h, v) in enumerate(((amp_h, amp), (om_h, om), (cpl_h, cpl), (inv_h, inv)))
+    ]
+
     def start(copies):
         for c in copies:
             c.start()
@@ -65,6 +71,7 @@
     start(fields[0][0])
     start(fields[1][1])
     start(fields[0][1])
+    start(params)
     start(smalls[2])
     start(smalls[1])
 
@@ -107,17 +114,21 @@
         d = den[x]
         return d * d * d
 
-    for f in range(F):
-        wait(fields[1][f])
-        halo(0, f, "start")
-        if f == 0:
-            wait(smalls[0])
+    def stiffened(f):
         wait(fields[0][f])
         for x in range(X):
             s = stiff(x)
             for c in range(2):
                 sp[f, x, c] = s * p[f, x, c]
-        halo(1, f, "start")
+
+    wait(fields[1][0])
+    halo(0, 0, "start")
+    wait(smalls[0])
+    stiffened(0)
+    halo(1, 0, "start")
+    for f in range(1, F):
+        wait(fields[1][f])
+        stiffened(f)
 
     for side in range(2):
 
@@ -126,6 +137,8 @@
             for kind in range(3):
                 for f in range(F):
                     hal[kind, f, side] = jnp.zeros((2, Q, N), jnp.float32)
+
+    wait(params)
 
     cs = [cpl[d] for d in range(7)]
     ct = [c.T for c in cs]
@@ -167,10 +180,7 @@
     def mass(w, re, im):
         return w * (re + BETA * im), w * (im - BETA * re)
 
-    wait(smalls[2])
-
-    def residuals(i, carry):
-        f, x = i // X, i % X
+    def residuals(x, carry, f):
         d = den[x]
         w = om[f] * d
         mp = mass(w, p[f, x, 0], p[f, x, 1])
@@ -181,42 +191,51 @@
             ra[f, x, c] = ma[c] - s * local_sum(1, a, f, x, c)
         return carry
 
-    lax.fori_loop(0, F * X, residuals, 0)
+    def sweep(x, carry, f):
+        r = [rp[f, x, c] - halo_sum(0, hal[1, f, x, c], x) for c in range(2)]
+        step = folded_dot(lp[0, f], jnp.concatenate(split(jnp.concatenate(r, axis=0)), axis=0))
+        new = [p[f, x, c] + step[c * Q:(c + 1) * Q] for c in range(2)]
+        s, o = stiff(x), obs[x]
+        r = [ra[f, x, c] - s * halo_sum(1, hal[0, f, x, c], x) - o * new[c] for c in range(2)]
+        step = folded_dot(lp[1, f], jnp.concatenate(split(jnp.concatenate(r, axis=0)), axis=0))
+        for c in range(2):
+            pn[f, x, c] = new[c]
+            an[f, x, c] = a[f, x, c] + step[c * Q:(c + 1) * Q]
+        return carry
+
+    def gradient(x, carry, f):
+        d = den[x]
+        pr, pi, ar, ai = pn[f, x, 0], pn[f, x, 1], an[f, x, 0], an[f, x, 1]
+        wr, wi = local_sum(1, an, f, x, 0), local_sum(1, an, f, x, 1)
+        total = (3.0 * d * d) * (pr * wr - pi * wi)
+        total = total - om[f] * ((ar * pr - ai * pi) + BETA * (ar * pi + ai * pr))
+        grad[x] = total if f == 0 else grad[x] + total
+        return carry
+
+    def planes(body, f):
+        lax.fori_loop(0, X, functools.partial(body, f=f), 0)
+
+    wait(smalls[2])
+    planes(residuals, 0)
+    for f in range(1, F):
+        halo(0, f - 1, "wait_send")
+        halo(0, f, "start")
+        planes(residuals, f)
+        halo(1, f - 1, "wait_send")
+        halo(1, f, "start")
     wait(smalls[1])
-
     for f in range(F):
         halo(0, f, "wait_recv")
         halo(1, f, "wait_recv")
-
-        def sweep(x, carry, f=f):
-            r = [rp[f, x, c] - halo_sum(0, hal[1, f, x, c], x) for c in range(2)]
-            step = folded_dot(lp[0, f], jnp.concatenate(split(jnp.concatenate(r, axis=0)), axis=0))
-            new = [p[f, x, c] + step[c * Q:(c + 1) * Q] for c in range(2)]
-            s, o = stiff(x), obs[x]
-            r = [ra[f, x, c] - s * halo_sum(1, hal[0, f, x, c], x) - o * new[c] for c in range(2)]
-            step = folded_dot(lp[1, f], jnp.concatenate(split(jnp.concatenate(r, axis=0)), axis=0))
-            for c in range(2):
-                pn[f, x, c] = new[c]
-                an[f, x, c] = a[f, x, c] + step[c * Q:(c + 1) * Q]
-            return carry
-
-        lax.fori_loop(0, X, sweep, 0)
+        planes(sweep, f)
+        if f == F - 2:
+            planes(gradient, f)
+            halo(0, F - 1, "wait_send")
+            halo(1, F - 1, "wait_send")
         for piece in range(PIECES):
             halo(2, f, "start", piece)
-
-    def gradient(x, carry):
-        d = den[x]
-        three = 3.0 * d * d
-        total = jnp.zeros((Q, N), jnp.float32)
-        for f in range(F):
-            pr, pi, ar, ai = pn[f, x, 0], pn[f, x, 1], an[f, x, 0], an[f, x, 1]
-            wr, wi = local_sum(1, an, f, x, 0), local_sum(1, an, f, x, 1)
-            total = total + three * (pr * wr - pi * wi)
-            total = total - om[f] * ((ar * pr - ai * pi) + BETA * (ar * pi + ai * pr))
-        grad[x] = total
-        return carry
-
-    lax.fori_loop(0, X, gradient, 0)
+        if f != F - 2:
+            planes(gradient, f)
 
     def share(k, piece):
         peer = lax.rem(me_f + k, nf)
@@ -252,8 +271,6 @@
     start(outs)
     wait(outs)
     for f in range(F):
-        halo(0, f, "wait_send")
-        halo(1, f, "wait_send")
         for piece in range(PIECES):
             halo(2, f, "wait_send", piece)
     for piece in range(PIECES):
@@ -267,16 +284,15 @@
     f32, bf16, dma = jnp.float32, jnp.bfloat16, pltpu.SemaphoreType.DMA
     field = pltpu.VMEM((F, X, 2, Q, N), f32)
     plane = pltpu.VMEM((X, Q, N), f32)
-    smem = pl.BlockSpec(memory_space=pltpu.SMEM)
-    vmem = pl.BlockSpec(memory_space=pltpu.VMEM)
-    anyw = pl.BlockSpec(memory_space=pl.ANY)
+    hbm = pl.BlockSpec(memory_space=pltpu.HBM)
     columns = F * X * 2 * N
     return pl.pallas_call(
         functools.partial(kernel, nf, nsx),
         out_shape=jax.ShapeDtypeStruct((rows, X, N), f32),
-        in_specs=[smem, smem, anyw, anyw, anyw, vmem, vmem, anyw, anyw],
-        out_specs=anyw,
+        in_specs=[hbm] * 9,
+        out_specs=hbm,
         scratch_shapes=[
+            pltpu.SMEM(amp.shape, f32), pltpu.SMEM(om.shape, f32), pltpu.VMEM(cpl.shape, f32), pltpu.VMEM(inv.shape, f32),
             plane, plane, plane,
             field, field, field, field, field, field, field,
             pltpu.VMEM((3, F, 2, 2, Q, N), f32),
@@ -286,13 +302,13 @@
             plane,
             pltpu.VMEM((nf - 1, X, rows, N), f32),
             pltpu.VMEM((X, rows, N), f32),
-            dma((3, X)), dma((2, F, X)),
+            dma((4,)), dma((3, X)), dma((2, F, X)),
             dma((3, F, 2, PIECES)), dma((3, F, 2, PIECES)),
             dma((nf - 1, PIECES)), dma((nf - 1, PIECES)),
             dma((X,)),
         ],
         compiler_params=pltpu.CompilerParams(
-            collective_id=0, has_side_effects=True, vmem_limit_bytes=48 * 1024 * 1024
+            collective_id=0, has_side_effects=True, vmem_limit_bytes=60 * 1024 * 1024
         ),
         cost_estimate=pl.CostEstimate(
             flops=2 * columns * (3 * 7 * Q * Q + 4 * Q * Q) * 3, bytes_accessed=4 * (2 * columns * Q), transcendentals=0

time: 55.1 us -> 45.4 us (0.82)
  local copies, waits for them, and re-layouts: 9.1 us -> 1.47 us
  Pallas kernels: 45.6 us -> 43.7 us
    unnamed x19 -> x1, local copies, waits for them, and re-layouts: 9.1 us -> 1.47 us
    pallas_call x1, Pallas kernels: 45.6 us -> 43.7 us  [shards(): pl.pallas_call(functools.partial(kernel, nf, nsx), out_shape=jax.ShapeDty...]
where the time goes in v1:
time: 45.4 us; the launch traced here: 45.2 us
  Pallas kernels  43.7 us (96%)
  local copies, waits for them, and re-layouts  1.47 us (3%)
    pallas_call x1, Pallas kernels, shards(): pl.pallas_call(functools.partial(kernel, nf, nsx), out_shape=jax.ShapeDty...  43.7 us
    unnamed x1, local copies, waits for them, and re-layouts  1.47 us

profile of v1, /device:TPU:0, one launch (start us, length us, event | category | flops | bytes accessed | tf_op | source)
XLA Modules:
  0.0 45.2 jit_solution(2923374700792728128)
XLA Ops:
  0.0 43.7 %shard_map.91 = f32[16,2,512]{2,1,0:T(2,128)} custom-call(f32[2,2]{1,0:T(2,128)} %amp_h.1, f32[2]{0:T(128)} %om_h.1, f32[64,2,512]{2,1,0:T(2,128)} %den_h.1, f32[64,2,512]{2,1,0:T(2,128)} %obs_h.1, f32[64,2,512]{2,1,0:T(2,128)} %src_h.1, f32[7,64,64]{2,1,0:T(8,128)} %cpl_h.1, f32[2,2,64,64]{3,2,1,0:T(8,128)} %inv_h.1, f32[2,2,64,2,512]{4,3,2,1,0:T(2,128)} %p_h.1, ...), custom_call_target="tpu_custom_call" | custom-call | flops 2516582400 | bytes 2097152 | tf_op jit(solution)/shard_map/pallas_call | solution.py:289
  43.7 1.5 %copy.11 = f32[16,2,512]{2,1,0:T(2,128)} copy(f32[16,2,512]{2,1,0:T(2,128)} %shard_map.91) | data formatting | bytes 131072

commit v2 on v1

--- a/solution.py
+++ b/solution.py
@@ -35,9 +35,9 @@
 def kernel(
     nf, nsx,
     amp_h, om_h, den_h, obs_h, src_h, cpl_h, inv_h, p_h, a_h,
-    out_h,
+    got,
     amp, om, cpl, inv,
-    den, obs, src, p, a, sp, pn, an, rp, ra, hal, lk, lh, lp, grad, got, osum,
+    den, obs, src, p, a, sp, pn, an, rp, ra, hal, lk, lh, lp, grad,
     param_sem, small_sem, field_sem, send_h, recv_h, send_g, recv_g, out_sem,
 ):
     F, X, _, Q, N = p.shape
@@ -212,6 +212,9 @@
         grad[x] = total if f == 0 else grad[x] + total
         return carry
 
+    def pieces(f):
+        return range(PIECES) if f == F - 1 else (None,)
+
     def planes(body, f):
         lax.fori_loop(0, X, functools.partial(body, f=f), 0)
 
@@ -232,7 +235,7 @@
             planes(gradient, f)
             halo(0, F - 1, "wait_send")
             halo(1, F - 1, "wait_send")
-        for piece in range(PIECES):
+        for piece in pieces(f):
             halo(2, f, "start", piece)
         if f != F - 2:
             planes(gradient, f)
@@ -248,8 +251,8 @@
         )
 
     for f in range(F):
-        for piece in range(PIECES):
-            cols = slice(piece * (N // PIECES), (piece + 1) * (N // PIECES))
+        for piece in pieces(f):
+            cols = slice(0, N) if piece is None else slice(piece * (N // PIECES), (piece + 1) * (N // PIECES))
             halo(2, f, "wait_recv", piece)
             for x in range(X):
                 d = den[x, :, cols]
@@ -258,20 +261,16 @@
             if f == F - 1:
                 for k in range(1, nf):
                     share(k, piece).start()
-
     mine = pl.ds(pl.multiple_of(me_f * rows, rows), rows)
+    own = pltpu.make_async_copy(grad.at[:, mine, :], got.at[nf - 1], out_sem)
+    own.start()
+
     for piece in range(PIECES):
-        cols = slice(piece * (N // PIECES), (piece + 1) * (N // PIECES))
-        total = grad[:, mine, cols]
         for k in range(1, nf):
             share(k, piece).wait_recv()
-            total = total + got[k - 1, :, :, cols]
-        osum[:, :, cols] = total
-    outs = [pltpu.make_async_copy(osum.at[x], out_h.at[:, x, :], out_sem.at[x]) for x in range(X)]
-    start(outs)
-    wait(outs)
+    own.wait()
     for f in range(F):
-        for piece in range(PIECES):
+        for piece in pieces(f):
             halo(2, f, "wait_send", piece)
     for piece in range(PIECES):
         for k in range(1, nf):
@@ -286,9 +285,9 @@
     plane = pltpu.VMEM((X, Q, N), f32)
     hbm = pl.BlockSpec(memory_space=pltpu.HBM)
     columns = F * X * 2 * N
-    return pl.pallas_call(
+    terms = pl.pallas_call(
         functools.partial(kernel, nf, nsx),
-        out_shape=jax.ShapeDtypeStruct((rows, X, N), f32),
+        out_shape=jax.ShapeDtypeStruct((nf, X, rows, N), f32),
         in_specs=[hbm] * 9,
         out_specs=hbm,
         scratch_shapes=[
@@ -300,12 +299,10 @@
             pltpu.VMEM((2, X, 2 * Q, 2 * Q), bf16),
             pltpu.VMEM((2, F, 4 * Q, 4 * Q), bf16),
             plane,
-            pltpu.VMEM((nf - 1, X, rows, N), f32),
-            pltpu.VMEM((X, rows, N), f32),
             dma((4,)), dma((3, X)), dma((2, F, X)),
             dma((3, F, 2, PIECES)), dma((3, F, 2, PIECES)),
             dma((nf - 1, PIECES)), dma((nf - 1, PIECES)),
-            dma((X,)),
+            dma,
         ],
         compiler_params=pltpu.CompilerParams(
             collective_id=0, has_side_effects=True, vmem_limit_bytes=60 * 1024 * 1024
@@ -314,6 +311,7 @@
             flops=2 * columns * (3 * 7 * Q * Q + 4 * Q * Q) * 3, bytes_accessed=4 * (2 * columns * Q), transcendentals=0
         ),
     )(amp, om, den, obs, src, cpl, inv, p, a)
+    return jnp.sum(terms, axis=0).transpose(1, 0, 2)
 
 
 def solution(mesh):

time: 45.4 us -> 45 us (level)
  other arithmetic: 0 us -> 0.98 us
  local copies, waits for them, and re-layouts: 1.47 us -> 0.68 us
  Pallas kernels: 43.7 us -> 43.2 us
    unnamed x1 -> x0, local copies, waits for them, and re-layouts: 1.47 us -> none
    reduce_sum x0 -> x1, other arithmetic: none -> 0.98 us  [shards(): return jnp.sum(terms, axis=0).transpose(1, 0, 2)]
    transpose x0 -> x1, local copies, waits for them, and re-layouts: none -> 0.68 us  [shards(): return jnp.sum(terms, axis=0).transpose(1, 0, 2)]
    pallas_call x1, Pallas kernels: 43.7 us -> 43.2 us  [shards(): pl.pallas_call(functools.partial(kernel, nf, nsx), out_shape=jax.ShapeDty...]
where the time goes in v2:
time: 45 us; the launch traced here: 44.9 us
  Pallas kernels  43.2 us (96%)
  other arithmetic  0.98 us (2%)
  local copies, waits for them, and re-layouts  0.68 us (2%)
    pallas_call x1, Pallas kernels, shards(): pl.pallas_call(functools.partial(kernel, nf, nsx), out_shape=jax.ShapeDty...  43.2 us
    reduce_sum x1, other arithmetic, shards(): return jnp.sum(terms, axis=0).transpose(1, 0, 2)  0.98 us

profile of v2, /device:TPU:0, one launch (start us, length us, event | category | flops | bytes accessed | tf_op | source)
XLA Modules:
  0.0 44.9 jit_solution(15522220047483560463)
XLA Ops:
  0.0 43.2 %shard_map.91 = f32[4,2,16,512]{3,2,1,0:T(8,128)} custom-call(f32[2,2]{1,0:T(2,128)} %amp_h.1, f32[2]{0:T(128)} %om_h.1, f32[64,2,512]{2,1,0:T(2,128)} %den_h.1, f32[64,2,512]{2,1,0:T(2,128)} %obs_h.1, f32[64,2,512]{2,1,0:T(2,128)} %src_h.1, f32[7,64,64]{2,1,0:T(8,128)} %cpl_h.1, f32[2,2,64,64]{3,2,1,0:T(8,128)} %inv_h.1, f32[2,2,64,2,512]{4,3,2,1,0:T(2,128)} %p_h.1, ...), custom_call_target="tpu_custom_call" | custom-call | flops 2516582400 | bytes 2097152 | tf_op jit(solution)/shard_map/pallas_call | solution.py:288
  43.2 1.0 %reduce_sum.9 = f32[2,16,512]{2,1,0:T(8,128)S(1)} reduce(f32[4,2,16,512]{3,2,1,0:T(8,128)} %shard_map.91, f32[]{:T(128)} %constant.0.clone.1), dimensions={0}, to_apply=%region_0.0 | reduce | flops 49152 | bytes 327684 | tf_op jit(solution)/shard_map/reduce_sum | solution.py:314
  44.2 0.7 %copy.10 = f32[16,2,512]{2,1,0:T(2,128)} copy(f32[16,2,512]{2,0,1:T(8,128)S(1)} %bitcast.1) | data formatting | bytes 131072 | tf_op jit(solution)/shard_map/transpose | solution.py:314
